TPU v7x, 256 devices: a whole 4x4x8 slice. The times are simulated.
256 devices in a mesh: seq: 32 (over y, z_hi, core), mp: 8 (over z_lo, x).
Axes of the slice: x: 4, y: 4, z: 8 (z_hi: 4, z_lo: 2; z = z_hi * 2 + z_lo), core: 2. Of those that a mesh axis runs over, the one named last changes fastest.
Arguments:
- frames_in: bfloat16 [5632, 1536], P(('seq', 'mp')), may hold values from -6 to 6
- attn_gain: float32 [1536], replicated, may hold values from 0.25 to 1.75
- attn_shift: float32 [1536], replicated, may hold values from -3 to 3
- w_qkv: bfloat16 [3, 1536, 1536], P(None, 'mp'), may hold values from -0.76546554 to 0.76546554
- w_attn_out: bfloat16 [1536, 1536], P('mp'), may hold values from -2.5 to 2.5
- conv_gain: float32 [1536], replicated, may hold values from 0.25 to 1.75
- conv_shift: float32 [1536], replicated, may hold values from -3 to 3
- w_pointwise_in: bfloat16 [2, 1536, 1536], P(None, 'mp'), may hold values from -0.15625 to 0.15625
- depth_kernel: float32 [31, 1536], P(None, 'mp'), may hold values from -2 to 2
- norm_scale: float32 [1536], P('mp'), may hold values from 0.5 to 2
- norm_offset: float32 [1536], P('mp'), may hold values from -3 to 3
- w_pointwise_out: bfloat16 [1536, 1536], P('mp'), may hold values from -0.15625 to 0.15625
Outputs:
- block_out: bfloat16 [5632, 1536], P(('seq', 'mp'))
All inputs are finite; a program needn't handle non-finite values.
Results may differ from a plain program's by a relative error of at most 0.018.
The roundings to bfloat16 on the way count: a program that leaves them out, or rounds other values in their place, can miss the bound.
Values may be sent and summed in bfloat16 or wider, within the bound.
No kernel may reach another device: no remote copies, remote signals or barrier semaphores. Data moves between devices by JAX's collectives and lax.ppermute only.
A program may use at most 64 MiB of HBM per device.

v0:
```python
import jax
import jax.numpy as jnp
from jax import lax
from jax.sharding import PartitionSpec as P

D = 1536
HEADS = 16


def padded_2(cells, sides, width):
    for axis, dim in sides:
        count = lax.axis_size(axis)
        ends = count - 1
        head = lax.slice_in_dim(cells, 0, width, axis=dim)
        tail = lax.slice_in_dim(cells, cells.shape[dim] - width, cells.shape[dim], axis=dim)
        cells = jnp.concatenate(
            [
                lax.ppermute(tail, axis, [(i, (i + 1) % count) for i in range(ends)]),
                cells,
                lax.ppermute(head, axis, [((i + 1) % count, i) for i in range(ends)]),
            ],
            axis=dim,
        )
    return cells


def layer_norm(values, gain, shift):
    vf = values.astype(jnp.float32)
    center = vf - jnp.mean(vf, axis=-1, keepdims=True)
    spread = jnp.mean(center * center, axis=-1, keepdims=True)
    return (center * lax.rsqrt(spread + 1e-05) * gain + shift).astype(jnp.bfloat16)


def rotate(tensor, positions):
    half = tensor.shape[-1] // 2
    freq = 10000.0 ** (-jnp.arange(half).astype(jnp.float32) / half)
    angle = positions.astype(jnp.float32)[:, None] * freq[None, :]
    cosine = jnp.cos(angle)[:, None, :]
    sine = jnp.sin(angle)[:, None, :]
    first = tensor[..., :half]
    second = tensor[..., half:]
    return jnp.concatenate(
        [first * cosine - second * sine, first * sine + second * cosine], axis=-1
    )


def project_out_in(inputs, weight):
    return lax.dot_general(
        inputs, weight, (((1,), (1,)), ((), ())), preferred_element_type=jnp.float32
    )


def attend_block(carry, queries, key_block, value_block, scale):
    run_max, run_total, run_acc = carry
    scores = (
        jnp.einsum("qhd,khd->qhk", queries, key_block, preferred_element_type=jnp.float32) * scale
    )
    new_max = jnp.maximum(run_max, jnp.max(scores, axis=-1))
    weights = jnp.exp(scores - new_max[..., None])
    decay = jnp.exp(run_max - new_max)
    new_total = run_total * decay + jnp.sum(weights, axis=-1)
    mixed = jnp.einsum(
        "qhk,khd->qhd",
        weights.astype(jnp.bfloat16),
        value_block,
        preferred_element_type=jnp.float32,
    )
    return (new_max, new_total, run_acc * decay[..., None] + mixed)


def attend(carry, queries, key_piece, value_piece, scale):
    count = key_piece.shape[0]
    blocks = 1
    key_steps = key_piece.reshape(blocks, count // blocks, key_piece.shape[1], key_piece.shape[2])
    value_steps = value_piece.reshape(
        blocks, count // blocks, value_piece.shape[1], value_piece.shape[2]
    )

    def step(state, pair):
        return (attend_block(state, queries, pair[0], pair[1], scale), None)

    result, unused = lax.scan(step, carry, (key_steps, value_steps))
    return result


def local(
    frames_in,
    attn_gain,
    attn_shift,
    w_qkv,
    w_attn_out,
    conv_gain,
    conv_shift,
    w_pointwise_in,
    depth_kernel,
    norm_scale,
    norm_offset,
    w_pointwise_out,
):
    local_width = w_qkv.shape[1]
    local_heads = HEADS // lax.axis_size("mp")
    head_dim = D // HEADS
    scale = 1.0 / head_dim**0.5
    whole_in = lax.all_gather(frames_in, "mp", axis=0, tiled=True)
    frame_count = whole_in.shape[0]
    attn_in = layer_norm(whole_in, attn_gain, attn_shift)
    positions = lax.axis_index("seq") * frame_count + jnp.arange(frame_count)
    projected = [
        project_out_in(attn_in, w_qkv[slot]).reshape(frame_count, local_heads, head_dim)
        for slot in range(3)
    ]
    queries = rotate(projected[0], positions).astype(jnp.bfloat16)
    keys = rotate(projected[1], positions).astype(jnp.bfloat16)
    values = projected[2].astype(jnp.bfloat16)
    start_state = (
        jnp.full((frame_count, local_heads), -1e30, jnp.float32),
        jnp.zeros((frame_count, local_heads), jnp.float32),
        jnp.zeros((frame_count, local_heads, head_dim), jnp.float32),
    )
    run_max, run_total, run_acc = attend(
        start_state,
        queries,
        lax.all_gather(keys, "seq", axis=0, tiled=True),
        lax.all_gather(values, "seq", axis=0, tiled=True),
        scale,
    )
    context = (
        (run_acc / run_total[..., None]).astype(jnp.bfloat16).reshape(frame_count, local_width)
    )
    partial_attn = jnp.dot(context, w_attn_out, preferred_element_type=jnp.float32)
    attn_part = lax.psum_scatter(
        partial_attn.astype(jnp.bfloat16), "mp", scatter_dimension=0, tiled=True
    ).astype(jnp.float32)
    mid = (frames_in.astype(jnp.float32) + attn_part).astype(jnp.bfloat16)
    whole_mid = lax.all_gather(mid, "mp", axis=0, tiled=True)
    conv_in = layer_norm(whole_mid, conv_gain, conv_shift)
    value_half = project_out_in(conv_in, w_pointwise_in[0])
    gate_half = project_out_in(conv_in, w_pointwise_in[1])
    glu = (value_half * jax.nn.sigmoid(gate_half)).astype(jnp.bfloat16)
    taps = depth_kernel.shape[0]
    padded = padded_2(glu, (("seq", 0),), taps // 2)
    depth = jnp.zeros((frame_count, local_width), jnp.float32)
    for tap in range(taps):
        depth = depth + padded[tap : tap + frame_count].astype(jnp.float32) * depth_kernel[tap]
    normed = depth * norm_scale + norm_offset
    swish = (normed * jax.nn.sigmoid(normed)).astype(jnp.bfloat16)
    partial_conv = jnp.dot(swish, w_pointwise_out, preferred_element_type=jnp.float32)
    conv_part = lax.psum_scatter(
        partial_conv.astype(jnp.bfloat16), "mp", scatter_dimension=0, tiled=True
    ).astype(jnp.float32)
    return (mid.astype(jnp.float32) + conv_part).astype(jnp.bfloat16)


def solution(mesh):
    placed = (
        P(("seq", "mp"), None),
        P(),
        P(),
        P(None, "mp", None),
        P("mp", None),
        P(),
        P(),
        P(None, "mp", None),
        P(None, "mp"),
        P("mp"),
        P("mp"),
        P("mp", None),
    )
    return jax.shard_map(
        local, mesh=mesh, in_specs=placed, out_specs=P(("seq", "mp"), None), check_vma=False
    )
```

profile of v0, /device:TPU:56, one launch (start us, length us, event | category | flops | bytes accessed | tf_op | source)
XLA Modules:
  0.0 273.2 jit_solution(18006487947794246170)
XLA Ops:
  6.5 29.5 %all-gather = bf16[8,22,1536]{2,1,0:T(8,128)(2,1)S(1)} all-gather(bf16[1,22,1536]{2,1,0:T(8,128)(2,1)} %bitcast.74), channel_id=1, replica_groups=mesh['seq'=32,'mp'=8] {'mp'}, dimensions={0}, use_global_device_ids=true | all-gather | bytes 608256 | tf_op jit(solution)/shard_map/all_gather | solution.py:104
  36.7 1.5 fusion.65
  39.9 0.7 pad_maximum_fusion.2
  40.8 1.0 convolution_convert_fusion.2
  41.8 56.4 %all-gather.5.cloned.1.call-done = bf16[5632,2,96]{2,0,1:T(8,128)(2,1)} async-done(((bf16[176,2,96]{2,0,1:T(8,128)(2,1)}), bf16[5632,2,96]{2,0,1:T(8,128)(2,1)}) %all-gather.5.cloned.1.call-update) | async-done | bytes 2162704 | tf_op jit(solution)/shard_map/all_gather | solution.py:123
  98.2 3.1 %fusion.69 = (f32[176,2]{0,1:T(2,128)S(1)}, f32[176,2,5632]{2,0,1:T(8,128)S(1)}) fusion(bf16[5632,2,96]{2,0,1:T(8,128)(2,1)} %all-gather.5.cloned.1.call-done, bf16[176,2,48]{2,0,1:T(8,128)(2,1)S(1)} %get-tuple-element.28, bf16[176,2,48]{2,0,1:T(8,128)(2,1)S(1)} %get-tuple-element.20), kind=kOutput, calls=%fused_computation.138 | convolution fusion | flops 384732832 | bytes 10161536 | tf_op jit(solution)/shard_map/while/body/eval_jaxpr/qhd,khd->qhk/dot_general | solution.py:56
  101.4 1.2 fusion.3
  102.6 1.9 copy-done.1
  104.5 50.5 %all-gather.7.cloned.1.call-done = bf16[5632,2,96]{2,0,1:T(8,128)(2,1)} async-done(((bf16[176,2,96]{2,0,1:T(8,128)(2,1)}), bf16[5632,2,96]{2,0,1:T(8,128)(2,1)}) %all-gather.7.cloned.1.call-update) | async-done | bytes 2162704 | tf_op jit(solution)/shard_map/all_gather | solution.py:124
  154.9 5.4 %fusion.21 = bf16[176,2,96]{2,0,1:T(8,128)(2,1)S(1)} fusion(bf16[5632,2,96]{2,0,1:T(8,128)(2,1)} %all-gather.7.cloned.1.call-done, f32[176,2,5632]{2,0,1:T(8,128)} %copy-done.1, f32[176,2]{0,1:T(2,128)S(1)} %broadcast_maximum_fusion, f32[176,2]{0,1:T(2,128)S(1)} %get-tuple-element.69, f32[176,2]{0,1:T(2,128)S(1)} %get-tuple-element.68), kind=kOutput, calls=%fused_computation.19 | convolution fusion | flops 384699392 | bytes 10164352 | tf_op jit(solution)/shard_map/while/body/eval_jaxpr/qhk,khd->qhd/dot_general | solution.py:62
  160.9 23.1 %fusion = bf16[24,1536]{1,0:T(8,128)(2,1)S(1)} fusion(bf16[176,1536]{1,0:T(8,128)(2,1)S(1)} %convolution_convert_fusion.1), kind=kCustom, calls=%all-reduce-scatter | all-reduce-scatter fusion | flops 294913 | bytes 615424
  184.1 3.4 %collective-permute-start.2 = (bf16[14,1536]{1,0:T(8,128)(2,1)S(1)}, bf16[14,1536]{1,0:T(8,128)(2,1)S(1)}, u32[]{:S(2)}, u32[]{:S(2)}) collective-permute-start(bf16[14,1536]{1,0:T(8,128)(2,1)S(1)} %slice.380), channel_id=1, source_target_pairs={{0,1},{1,2},{2,3},{3,4},{4,5},{5,6},{6,7},{8,9},{9,10},{10,11},{11... | collective-permute-start | bytes 129032
  187.6 0.6 dynamic-slice.8
  188.8 3.4 %collective-permute-done.2 = bf16[14,1536]{1,0:T(8,128)(2,1)S(1)} collective-permute-done((bf16[14,1536]{1,0:T(8,128)(2,1)S(1)}, bf16[14,1536]{1,0:T(8,128)(2,1)S(1)}, u32[]{:S(2)}, u32[]{:S(2)}) %collective-permute-start.2) | collective-permute-done | bytes 43040
  192.4 29.3 %all-gather.1 = bf16[8,22,1536]{2,1,0:T(8,128)(2,1)S(1)} all-gather(bf16[1,22,1536]{2,1,0:T(8,128)(2,1)S(1)} %fusion.60), channel_id=1, replica_groups=mesh['seq'=32,'mp'=8] {'mp'}, dimensions={0}, use_global_device_ids=true | all-gather | bytes 608256 | tf_op jit(solution)/shard_map/all_gather | solution.py:135
  222.5 1.6 fusion.10
  224.5 1.9 collective-permute-start
  226.5 6.7 %collective-permute-start.1 = (bf16[15,192]{1,0:T(8,128)(2,1)S(1)}, bf16[15,192]{1,0:T(8,128)(2,1)S(1)}, u32[]{:S(2)}, u32[]{:S(2)}) collective-permute-start(bf16[15,192]{1,0:T(8,128)(2,1)S(1)} %get-tuple-element.36), channel_id=1, source_target_pairs={{8,0},{16,8},{24,16},{32,24},{40,32},{48,40},{56,48},{64,56},{72,6... | collective-permute-start | bytes 17288 | tf_op jit(solution)/shard_map/ppermute | solution.py:20
  233.2 1.3 collective-permute-done.1
  234.5 1.0 convolution_convert_fusion
  235.5 21.8 %fusion.1 = bf16[24,1536]{1,0:T(8,128)(2,1)S(1)} fusion(bf16[176,1536]{1,0:T(8,128)(2,1)S(1)} %convolution_convert_fusion), kind=kCustom, calls=%all-reduce-scatter.1 | all-reduce-scatter fusion | flops 294913 | bytes 615424
  257.4 2.0 collective-permute-start.3
  259.3 6.1 %collective-permute-done.3 = bf16[14,1536]{1,0:T(8,128)(2,1)S(1)} collective-permute-done((bf16[14,1536]{1,0:T(8,128)(2,1)S(1)}, bf16[14,1536]{1,0:T(8,128)(2,1)S(1)}, u32[]{:S(2)}, u32[]{:S(2)}) %collective-permute-start.3) | collective-permute-done | bytes 43040
  265.6 0.7 add_convert_fusion.4
  (63 shorter events, 4.5 us)
Async XLA Ops:
  6.5 154.1 %copy-start = (bf16[192,1536]{1,0:T(8,128)(2,1)S(1)}, bf16[192,1536]{1,0:T(8,128)(2,1)}, u32[]{:S(2)}) copy-start(bf16[192,1536]{1,0:T(8,128)(2,1)} %param.16) | copy-start | bytes 1769476
  6.5 91.7 %all-gather.5.cloned.1.call-start = ((), (), s32[]{:S(2)}) async-start(), calls=%async_computation | async-start | bytes 2973696 | tf_op jit(solution)/shard_map/all_gather | solution.py:123
  36.7 1.6 copy-start.4
  36.7 1.6 copy-start.5
  40.7 114.2 %all-gather.7.cloned.1.call-start = ((), (), s32[]{:S(2)}) async-start(), calls=%async_computation.1 | async-start | bytes 2973696 | tf_op jit(solution)/shard_map/all_gather | solution.py:124
  101.4 3.1 %copy-start.1 = (f32[176,2,5632]{2,0,1:T(8,128)}, f32[176,2,5632]{2,0,1:T(8,128)S(1)}, u32[]{:S(2)}) copy-start(f32[176,2,5632]{2,0,1:T(8,128)S(1)} %get-tuple-element.73) | copy-start | bytes 23789572
  160.5 27.0 %copy-start.3 = (f32[31,192]{1,0:T(8,128)S(1)}, f32[31,192]{1,0:T(8,128)}, u32[]{:S(2)}) copy-start(f32[31,192]{1,0:T(8,128)} %param.20) | copy-start | bytes 71428
  160.5 27.1 %copy-start.6 = (u32[256]{0:T(256)S(1)}, u32[256]{0:T(256)}, u32[]{:S(2)}) copy-start(u32[256]{0:T(256)} %constant.48) | copy-start | bytes 3076
  160.6 31.8 %copy-start.2 = (bf16[22,1536]{1,0:T(8,128)(2,1)S(1)}, bf16[22,1536]{1,0:T(8,128)(2,1)}, u32[]{:S(2)}) copy-start(bf16[22,1536]{1,0:T(8,128)(2,1)} %param.12) | copy-start | bytes 202756
  184.1 8.1 %collective-permute-start.2 = (bf16[14,1536]{1,0:T(8,128)(2,1)S(1)}, bf16[14,1536]{1,0:T(8,128)(2,1)S(1)}, u32[]{:S(2)}, u32[]{:S(2)}) collective-permute-start(bf16[14,1536]{1,0:T(8,128)(2,1)S(1)} %slice.380), channel_id=1, source_target_pairs={{0,1},{1,2},{2,3},{3,4},{4,5},{5,6},{6,7},{8,9},{9,10},{10,11},{11... | collective-permute-start | bytes 129032
  221.8 0.7 copy-start.9
  221.8 0.7 copy-start.10
  222.5 1.6 copy-start.7
  224.1 10.4 %copy-start.8 = (bf16[192,1536]{1,0:T(8,128)(2,1)S(1)}, bf16[192,1536]{1,0:T(8,128)(2,1)}, u32[]{:S(2)}) copy-start(bf16[192,1536]{1,0:T(8,128)(2,1)} %param.23) | copy-start | bytes 1769476
  224.1 10.4 %copy-start.11 = (f32[192]{0:T(256)S(1)}, f32[192]{0:T(256)}, u32[]{:S(2)}) copy-start(f32[192]{0:T(256)} %param.22) | copy-start | bytes 2308
  224.1 10.3 %copy-start.12 = (f32[192]{0:T(256)S(1)}, f32[192]{0:T(256)}, u32[]{:S(2)}) copy-start(f32[192]{0:T(256)} %param.21) | copy-start | bytes 2308
  224.5 8.6 %collective-permute-start = (bf16[15,192]{1,0:T(8,128)(2,1)S(1)}, bf16[15,192]{1,0:T(8,128)(2,1)S(1)}, u32[]{:S(2)}, u32[]{:S(2)}) collective-permute-start(bf16[15,192]{1,0:T(8,128)(2,1)S(1)} %get-tuple-element.35), channel_id=1, source_target_pairs={{0,8},{8,16},{16,24},{24,32},{32,40},{40,48},{48,56},{56,64},{64,7... | collective-permute-start | bytes 17288 | tf_op jit(solution)/shard_map/ppermute | solution.py:18
  226.5 8.0 %collective-permute-start.1 = (bf16[15,192]{1,0:T(8,128)(2,1)S(1)}, bf16[15,192]{1,0:T(8,128)(2,1)S(1)}, u32[]{:S(2)}, u32[]{:S(2)}) collective-permute-start(bf16[15,192]{1,0:T(8,128)(2,1)S(1)} %get-tuple-element.36), channel_id=1, source_target_pairs={{8,0},{16,8},{24,16},{32,24},{40,32},{48,40},{56,48},{64,56},{72,6... | collective-permute-start | bytes 17288 | tf_op jit(solution)/shard_map/ppermute | solution.py:20
  257.4 8.1 %collective-permute-start.3 = (bf16[14,1536]{1,0:T(8,128)(2,1)S(1)}, bf16[14,1536]{1,0:T(8,128)(2,1)S(1)}, u32[]{:S(2)}, u32[]{:S(2)}) collective-permute-start(bf16[14,1536]{1,0:T(8,128)(2,1)S(1)} %slice.381), channel_id=1, source_target_pairs={{0,1},{1,2},{2,3},{3,4},{4,5},{5,6},{6,7},{8,9},{9,10},{10,11},{11... | collective-permute-start | bytes 129032
Sparse Core Ops, SparseCore 0:
  40.8 57.3 all-gather.4
  100.9 54.0 all-gather.6
where the time goes:
time: 274 us; the launch traced here: 273 us
  waiting for transfers between devices  118 us (43%)
  blocking collectives  104 us (38%)
  between operations  14.5 us (5%)
  starting transfers between devices  14 us (5%)
  matrix products  13.6 us (5%)
  local copies, waits for them, and re-layouts  5.21 us (2%)
  other arithmetic  4.42 us (2%)
    all_gather x1, waiting for transfers between devices, local(): lax.all_gather(keys, 'seq', axis=0, tiled=True)  56.4 us
    all_gather x1, waiting for transfers between devices, local(): lax.all_gather(values, 'seq', axis=0, tiled=True)  50.5 us
    unnamed x2, blocking collectives  44.9 us
    all_gather x1, blocking collectives, local(): whole_in = lax.all_gather(frames_in, 'mp', axis=0, tiled=True)  29.5 us
    all_gather x1, blocking collectives, local(): whole_mid = lax.all_gather(mid, 'mp', axis=0, tiled=True)  29.3 us
    unnamed x4, waiting for transfers between devices  9.55 us
    ppermute x1, starting transfers between devices, padded_2(): lax.ppermute(head, axis, [((i + 1) % count, i) for i in range(ends)])  6.65 us
  transfers between devices with their start and end apart: 6, of which 5 were waited for; matrix products, arithmetic and copies ran while one was open for 2% of the time, Pallas kernels for 0%

commit v1 on v0

--- a/solution.py
+++ b/solution.py
@@ -2,6 +2,7 @@
 import jax.numpy as jnp
 from jax import lax
 from jax.sharding import PartitionSpec as P
+from jax.lax import all_to_all, axis_size
 
 D = 1536
 HEADS = 16
@@ -117,11 +118,18 @@
         jnp.zeros((frame_count, local_heads), jnp.float32),
         jnp.zeros((frame_count, local_heads, head_dim), jnp.float32),
     )
+
+    def _advance_stocks(s0, comm_axis, at_axis):
+        oldest = axis_size(comm_axis)
+        v_now = jnp.stack([s0] * oldest)
+        lower = all_to_all(v_now, comm_axis, 0, 0)
+        return jnp.concatenate(lower, axis=at_axis)
+
     run_max, run_total, run_acc = attend(
         start_state,
         queries,
         lax.all_gather(keys, "seq", axis=0, tiled=True),
-        lax.all_gather(values, "seq", axis=0, tiled=True),
+        _advance_stocks(values, "seq", at_axis=0),
         scale,
     )
     context = (

time: 274 us -> 260 us (0.949)
  waiting for transfers between devices: 118 us -> 85.2 us
  local copies, waits for them, and re-layouts: 5.21 us -> 18 us
  starting transfers between devices: 14 us -> 19.6 us
    all_to_all x0 -> x1, waiting for transfers between devices: none -> 69.4 us  [_advance_stocks(): lower = all_to_all(v_now, comm_axis, 0, 0)]
    all_gather x1, waiting for transfers between devices: 56.4 us -> 0.02 us  [local(): lax.all_gather(keys, 'seq', axis=0, tiled=True)]
    all_gather x1 -> x0, waiting for transfers between devices: 50.5 us -> none  [local(): lax.all_gather(values, 'seq', axis=0, tiled=True)]
    all_to_all x0 -> x1, starting transfers between devices: none -> 10.6 us  [_advance_stocks(): lower = all_to_all(v_now, comm_axis, 0, 0)]
    squeeze x0 -> x1, local copies, waits for them, and re-layouts: none -> 5.67 us  [attend(): result, unused = lax.scan(step, carry, (key_steps, value_steps))]
    ppermute x1, waiting for transfers between devices: 0.01 us -> 5.53 us  [padded_2(): lax.ppermute(tail, axis, [(i, (i + 1) % count) for i in range(ends)])]
    all_to_all x0 -> x1, local copies, waits for them, and re-layouts: none -> 5.25 us  [_advance_stocks(): lower = all_to_all(v_now, comm_axis, 0, 0)]
    ppermute x1, starting transfers between devices: 6.65 us -> 1.92 us  [padded_2(): lax.ppermute(head, axis, [((i + 1) % count, i) for i in range(ends)])]
  transfers between devices with their start and end apart: 6 -> 6, of which waited for: 5 -> 4; matrix products, arithmetic and copies ran while one was open for 2% -> 7% of each run, Pallas kernels for 0% -> 0%
where the time goes in v1:
time: 260 us; the launch traced here: 259 us
  blocking collectives  104 us (40%)
  waiting for transfers between devices  85.2 us (33%)
  starting transfers between devices  19.6 us (8%)
  local copies, waits for them, and re-layouts  18 us (7%)
  between operations  14.5 us (6%)
  matrix products  12.1 us (5%)
  other arithmetic  5.07 us (2%)
    all_to_all x1, waiting for transfers between devices, _advance_stocks(): lower = all_to_all(v_now, comm_axis, 0, 0)  69.4 us
    unnamed x2, blocking collectives  45.5 us
    all_gather x1, blocking collectives, local(): whole_in = lax.all_gather(frames_in, 'mp', axis=0, tiled=True)  29.5 us
    all_gather x1, blocking collectives, local(): whole_mid = lax.all_gather(mid, 'mp', axis=0, tiled=True)  29.1 us
    all_to_all x1, starting transfers between devices, _advance_stocks(): lower = all_to_all(v_now, comm_axis, 0, 0)  10.6 us
    unnamed x3, waiting for transfers between devices  10.3 us
    dot_general x5, matrix products, project_out_in(): lax.dot_general(inputs, weight, (((1,), (1,)), ((), ())), preferred_eleme...  6.18 us
    squeeze x1, local copies, waits for them, and re-layouts, attend(): result, unused = lax.scan(step, carry, (key_steps, value_steps))  5.67 us
  transfers between devices with their start and end apart: 6, of which 4 were waited for; matrix products, arithmetic and copies ran while one was open for 7% of the time, Pallas kernels for 0%

profile of v1, /device:TPU:56, one launch (start us, length us, event | category | flops | bytes accessed | tf_op | source)
XLA Modules:
  0.0 258.6 jit_solution(9921146367573208520)
XLA Ops:
  6.5 29.5 %all-gather = bf16[8,22,1536]{2,1,0:T(8,128)(2,1)S(1)} all-gather(bf16[1,22,1536]{2,1,0:T(8,128)(2,1)} %bitcast.78), channel_id=1, replica_groups=mesh['seq'=32,'mp'=8] {'mp'}, dimensions={0}, use_global_device_ids=true | all-gather | bytes 608256 | tf_op jit(solution)/shard_map/all_gather | solution.py:105
  36.7 2.6 fusion.65
  40.7 2.0 stack.2
  42.7 10.6 %all-to-all-start = ((bf16[32,176,2,96]{3,1,2,0:T(8,128)(2,1)}), bf16[32,176,2,96]{3,1,2,0:T(8,128)(2,1)S(1)}, u32[]{:S(2)}, u32[]{:S(2)}) async-start(bf16[32,176,2,96]{3,1,2,0:T(8,128)(2,1)} %stack.2), calls=%async_computation | async-start | bytes 5767168 | tf_op jit(solution)/shard_map/all_to_all | solution.py:125
  53.4 2.3 fusion.71
  55.6 1.6 fusion.70
  59.3 69.4 %all-to-all-done = bf16[32,176,2,96]{3,1,2,0:T(8,128)(2,1)S(1)} async-done(((bf16[32,176,2,96]{3,1,2,0:T(8,128)(2,1)}), bf16[32,176,2,96]{3,1,2,0:T(8,128)(2,1)S(1)}, u32[]{:S(2)}, u32[]{:S(2)}) %all-to-all-start) | async-done | bytes 2162720 | tf_op jit(solution)/shard_map/all_to_all | solution.py:125
  128.6 5.2 %copy.16 = bf16[32,176,2,96]{1,0,3,2:T(8,128)(2,1)} copy(bf16[32,176,2,96]{3,1,2,0:T(8,128)(2,1)S(1)} %all-to-all-done) | data formatting | bytes 4325376 | tf_op jit(solution)/shard_map/all_to_all | solution.py:125
  133.9 5.7 %squeeze.16 = bf16[5632,2,96]{0,2,1:T(8,128)(2,1)S(1)} reshape(bf16[32,176,2,96]{1,0,3,2:T(8,128)(2,1)} %copy.16) | data formatting | bytes 4325376 | tf_op jit(solution)/shard_map/while/body/jit(dynamic_index_in_dim)/squeeze | solution.py:83
  139.6 3.1 %fusion.69 = (f32[176,2]{0,1:T(2,128)S(1)}, f32[176,2,5632]{2,0,1:T(8,128)S(1)}) fusion(bf16[5632,2,96]{2,0,1:T(8,128)(2,1)} %all-gather.4.cloned.1.call-done, bf16[176,2,48]{2,0,1:T(8,128)(2,1)S(1)} %copy-done.5, bf16[176,2,48]{2,0,1:T(8,128)(2,1)S(1)} %copy-done.4), kind=kOutput, calls=%fused_computation.138 | convolution fusion | flops 384732832 | bytes 10161536 | tf_op jit(solution)/shard_map/while/body/eval_jaxpr/qhd,khd->qhk/dot_general | solution.py:57
  142.8 1.2 fusion.3
  144.0 1.4 fusion.21
  146.0 23.3 %fusion = bf16[24,1536]{1,0:T(8,128)(2,1)S(1)} fusion(bf16[176,1536]{1,0:T(8,128)(2,1)S(1)} %convolution_convert_fusion.1), kind=kCustom, calls=%all-reduce-scatter | all-reduce-scatter fusion | flops 294913 | bytes 615424
  169.3 2.4 collective-permute-start.2
  173.0 4.4 %collective-permute-done.2 = bf16[14,1536]{1,0:T(8,128)(2,1)S(1)} collective-permute-done((bf16[14,1536]{1,0:T(8,128)(2,1)S(1)}, bf16[14,1536]{1,0:T(8,128)(2,1)S(1)}, u32[]{:S(2)}, u32[]{:S(2)}) %collective-permute-start.2) | collective-permute-done | bytes 43040
  177.6 29.1 %all-gather.1 = bf16[8,22,1536]{2,1,0:T(8,128)(2,1)S(1)} all-gather(bf16[1,22,1536]{2,1,0:T(8,128)(2,1)S(1)} %fusion.60), channel_id=1, replica_groups=mesh['seq'=32,'mp'=8] {'mp'}, dimensions={0}, use_global_device_ids=true | all-gather | bytes 608256 | tf_op jit(solution)/shard_map/all_gather | solution.py:143
  207.6 1.5 fusion.13
  209.6 1.9 collective-permute-start.1
  211.5 2.4 collective-permute-start
  214.0 5.5 %collective-permute-done = bf16[15,192]{1,0:T(8,128)(2,1)S(1)} collective-permute-done((bf16[15,192]{1,0:T(8,128)(2,1)S(1)}, bf16[15,192]{1,0:T(8,128)(2,1)S(1)}, u32[]{:S(2)}, u32[]{:S(2)}) %collective-permute-start) | collective-permute-done | bytes 5792 | tf_op jit(solution)/shard_map/ppermute | solution.py:19
  219.5 1.1 convolution_convert_fusion
  220.6 22.2 %fusion.1 = bf16[24,1536]{1,0:T(8,128)(2,1)S(1)} fusion(bf16[176,1536]{1,0:T(8,128)(2,1)S(1)} %convolution_convert_fusion), kind=kCustom, calls=%all-reduce-scatter.1 | all-reduce-scatter fusion | flops 294913 | bytes 615424
  242.8 2.2 collective-permute-start.3
  245.0 5.9 %collective-permute-done.3 = bf16[14,1536]{1,0:T(8,128)(2,1)S(1)} collective-permute-done((bf16[14,1536]{1,0:T(8,128)(2,1)S(1)}, bf16[14,1536]{1,0:T(8,128)(2,1)S(1)}, u32[]{:S(2)}, u32[]{:S(2)}) %collective-permute-start.3) | collective-permute-done | bytes 43040
  (71 shorter events, 7.6 us)
Async XLA Ops:
  6.5 139.1 %copy-start = (bf16[192,1536]{1,0:T(8,128)(2,1)S(1)}, bf16[192,1536]{1,0:T(8,128)(2,1)}, u32[]{:S(2)}) copy-start(bf16[192,1536]{1,0:T(8,128)(2,1)} %param.16) | copy-start | bytes 1769476
  36.7 2.6 %copy-start.7 = (f32[1536]{0:T(1024)S(1)}, f32[1536]{0:T(1024)}, u32[]{:S(2)}) copy-start(f32[1536]{0:T(1024)} %param.14) | copy-start | bytes 18436
  36.7 2.6 copy-start.8
  39.6 0.8 copy-start.1
  42.7 85.9 %all-to-all-start = ((bf16[32,176,2,96]{3,1,2,0:T(8,128)(2,1)}), bf16[32,176,2,96]{3,1,2,0:T(8,128)(2,1)S(1)}, u32[]{:S(2)}, u32[]{:S(2)}) async-start(bf16[32,176,2,96]{3,1,2,0:T(8,128)(2,1)} %stack.2), calls=%async_computation | async-start | bytes 5767168 | tf_op jit(solution)/shard_map/all_to_all | solution.py:125
  53.3 86.3 %all-gather.4.cloned.1.call-start = ((), (), s32[]{:S(2)}) async-start(), calls=%async_computation.1 | async-start | bytes 2973696 | tf_op jit(solution)/shard_map/all_gather | solution.py:131
  55.6 2.0 copy-start.2
  133.9 5.7 %copy-start.4 = (bf16[176,2,48]{2,0,1:T(8,128)(2,1)S(1)}, bf16[176,2,48]{2,0,1:T(8,128)(2,1)}, u32[]{:S(2)}) copy-start(bf16[176,2,48]{2,0,1:T(8,128)(2,1)} %get-tuple-element.20) | copy-start | bytes 101380
  133.9 5.7 %copy-start.5 = (bf16[176,2,48]{2,0,1:T(8,128)(2,1)S(1)}, bf16[176,2,48]{2,0,1:T(8,128)(2,1)}, u32[]{:S(2)}) copy-start(bf16[176,2,48]{2,0,1:T(8,128)(2,1)} %get-tuple-element.28) | copy-start | bytes 101380
  145.5 26.2 %copy-start.6 = (f32[31,192]{1,0:T(8,128)S(1)}, f32[31,192]{1,0:T(8,128)}, u32[]{:S(2)}) copy-start(f32[31,192]{1,0:T(8,128)} %param.20) | copy-start | bytes 71428
  145.5 26.3 %copy-start.9 = (u32[256]{0:T(256)S(1)}, u32[256]{0:T(256)}, u32[]{:S(2)}) copy-start(u32[256]{0:T(256)} %constant.48) | copy-start | bytes 3076
  145.7 31.9 %copy-start.3 = (bf16[22,1536]{1,0:T(8,128)(2,1)S(1)}, bf16[22,1536]{1,0:T(8,128)(2,1)}, u32[]{:S(2)}) copy-start(bf16[22,1536]{1,0:T(8,128)(2,1)} %param.12) | copy-start | bytes 202756
  169.3 8.1 %collective-permute-start.2 = (bf16[14,1536]{1,0:T(8,128)(2,1)S(1)}, bf16[14,1536]{1,0:T(8,128)(2,1)S(1)}, u32[]{:S(2)}, u32[]{:S(2)}) collective-permute-start(bf16[14,1536]{1,0:T(8,128)(2,1)S(1)} %slice.380), channel_id=1, source_target_pairs={{0,1},{1,2},{2,3},{3,4},{4,5},{5,6},{6,7},{8,9},{9,10},{10,11},{11... | collective-permute-start | bytes 129032
  206.9 0.7 copy-start.12
  206.9 0.7 copy-start.13
  207.6 1.6 copy-start.10
  209.2 10.3 %copy-start.11 = (bf16[192,1536]{1,0:T(8,128)(2,1)S(1)}, bf16[192,1536]{1,0:T(8,128)(2,1)}, u32[]{:S(2)}) copy-start(bf16[192,1536]{1,0:T(8,128)(2,1)} %param.23) | copy-start | bytes 1769476
  209.2 10.3 %copy-start.14 = (f32[192]{0:T(256)S(1)}, f32[192]{0:T(256)}, u32[]{:S(2)}) copy-start(f32[192]{0:T(256)} %param.22) | copy-start | bytes 2308
  209.2 10.3 %copy-start.15 = (f32[192]{0:T(256)S(1)}, f32[192]{0:T(256)}, u32[]{:S(2)}) copy-start(f32[192]{0:T(256)} %param.21) | copy-start | bytes 2308
  209.6 4.4 %collective-permute-start.1 = (bf16[15,192]{1,0:T(8,128)(2,1)S(1)}, bf16[15,192]{1,0:T(8,128)(2,1)S(1)}, u32[]{:S(2)}, u32[]{:S(2)}) collective-permute-start(bf16[15,192]{1,0:T(8,128)(2,1)S(1)} %get-tuple-element.36), channel_id=1, source_target_pairs={{8,0},{16,8},{24,16},{32,24},{40,32},{48,40},{56,48},{64,56},{72,6... | collective-permute-start | bytes 17288 | tf_op jit(solution)/shard_map/ppermute | solution.py:21
  211.5 8.0 %collective-permute-start = (bf16[15,192]{1,0:T(8,128)(2,1)S(1)}, bf16[15,192]{1,0:T(8,128)(2,1)S(1)}, u32[]{:S(2)}, u32[]{:S(2)}) collective-permute-start(bf16[15,192]{1,0:T(8,128)(2,1)S(1)} %get-tuple-element.35), channel_id=1, source_target_pairs={{0,8},{8,16},{16,24},{24,32},{32,40},{40,48},{48,56},{56,64},{64,7... | collective-permute-start | bytes 17288 | tf_op jit(solution)/shard_map/ppermute | solution.py:19
  242.8 8.1 %collective-permute-start.3 = (bf16[14,1536]{1,0:T(8,128)(2,1)S(1)}, bf16[14,1536]{1,0:T(8,128)(2,1)S(1)}, u32[]{:S(2)}, u32[]{:S(2)}) collective-permute-start(bf16[14,1536]{1,0:T(8,128)(2,1)S(1)} %slice.381), channel_id=1, source_target_pairs={{0,1},{1,2},{2,3},{3,4},{4,5},{5,6},{6,7},{8,9},{9,10},{10,11},{11... | collective-permute-start | bytes 129032
Sparse Core Ops, SparseCore 0:
  59.4 77.7 all-gather.3
